TPU v7x, 512 devices: a whole 4x8x8 slice. The times are simulated.
512 devices in a mesh: row: 64 (over y, x, core), rep: 8 (over z).
Axes of the slice: x: 4, y: 8, z: 8, core: 2. Of those that a mesh axis runs over, the one named last changes fastest.
Arguments:
- features: bfloat16 [32768, 768], P('row'), may hold values from -6 to 6
- order: int32 [32768], P('row'), may hold values from 0 to 32767, as said below
- adj_values: bfloat16 [256, 64, 3, 128, 128], P('row', 'rep'), may hold values from 0 to 0.044189453
- adj_cols: int32 [256, 64, 3], P('row', 'rep'), may hold values from 0 to 3, as said below
- adj_count: int32 [256, 64], P('row', 'rep'), may hold values from 0 to 3, as said below
- weight: bfloat16 [768, 1024], P(None, 'rep'), may hold values from -0.21875 to 0.21875
Outputs:
- hidden_out: bfloat16 [32768, 1024], P(('row', 'rep'))
Inputs may be any that keep to these rules, and one draw needn't show every extreme that they name: order[n] lies in the same slab of 512 nodes as n; each slab's entries are a permutation of that slab. `adj_cols`: the 3 entries of one row block and source slab are different block indices. `adj_count`: every row block has 3 live slots for its own slab; some source slabs have none.
All inputs are finite; a program needn't handle non-finite values.
Results may differ from a plain program's by a relative error of at most 0.0049.
Values may be sent and summed in bfloat16 or wider, within the bound.
A program may use at most 128 MiB of HBM per device.

v0:
```python
import jax
import jax.numpy as jnp
from jax import lax
from jax.sharding import PartitionSpec as P


def broadcast(x, axis, root):
    mine = lax.axis_index(axis) == root
    return lax.psum(jnp.where(mine, x, jnp.zeros_like(x)), axis)


def shards(features, order, adj_values, adj_cols, adj_count, weight):
    slab_rows = features.shape[0]
    feature_width = features.shape[1]
    block_size = adj_values.shape[-1]
    row_blocks = slab_rows // block_size
    sections = adj_values.shape[1]
    local_order = jnp.remainder(order, slab_rows)
    ordered = features[local_order]
    live_slots = (
        lax.broadcasted_iota(jnp.int32, adj_cols.shape, 2) < adj_count[:, :, None]
    ).astype(jnp.bfloat16)
    masked = adj_values * live_slots[:, :, :, None, None]
    rep_index = lax.axis_index("rep")
    running = jnp.zeros((row_blocks, block_size, feature_width), jnp.float32)
    for section in range(sections):
        slab_data = broadcast(ordered, "row", rep_index * sections + section)
        pieces = slab_data.reshape(row_blocks, block_size, feature_width)
        chosen = pieces[adj_cols[:, section]]
        running = running + jnp.einsum(
            "rkij,rkjd->rid", masked[:, section], chosen, preferred_element_type=jnp.float32
        )
    partial_r = running.reshape(slab_rows, feature_width)
    positions = lax.broadcasted_iota(jnp.int32, (slab_rows,), 0)
    inverse = jnp.zeros_like(local_order).at[local_order].set(positions)
    partial_orig = partial_r[inverse]
    row_share = lax.psum_scatter(partial_orig, "rep", scatter_dimension=0, tiled=True)
    whole_weight = lax.all_gather(weight, "rep", axis=1, tiled=True)
    product = jnp.dot(
        row_share.astype(jnp.bfloat16), whole_weight, preferred_element_type=jnp.float32
    )
    result = jax.nn.relu(product).astype(jnp.bfloat16)
    return result


def solution(mesh):
    placed = (
        P("row", None),
        P("row"),
        P("row", "rep", None, None, None),
        P("row", "rep", None),
        P("row", "rep"),
        P(None, "rep"),
    )
    return jax.shard_map(
        shards, mesh=mesh, in_specs=placed, out_specs=P(("row", "rep"), None), check_vma=False
    )
```

profile of v0, /device:TPU:1, one launch (start us, length us, event | category | flops | bytes accessed | tf_op | source)
XLA Modules:
  0.0 320.1 jit_solution(8990654134580150079)
XLA Ops:
  7.4 0.0 copy-start
  7.4 0.0 all-reduce.3.cloned.1.call-start
  7.4 0.8 compare_select_fusion.9
  8.1 0.4 copy-done
  8.5 2.0 gather_fusion
  10.5 2.9 broadcast_select_fusion
  13.5 0.0 all-reduce.3.cloned.1.call-update
  13.5 0.0 all-gather.2.cloned.1.call-start
  13.5 0.5 all-gather.2.cloned.1.call-update
  14.1 0.0 reduce-scatter.2.cloned.1.call-start
  14.1 0.0 copy-done.8
  14.2 0.6 slice_reduce_fusion
  14.7 0.1 copy.24
  14.8 0.1 reshape.316
  14.9 0.0 copy-done.9
  14.9 0.1 copy.17
  15.0 0.1 fusion.9
  15.1 0.1 copy.23
  15.2 0.1 reshape.308
  15.3 0.1 copy.22
  15.4 0.1 reshape.300
  15.5 0.1 copy.21
  15.6 0.1 reshape.292
  15.7 0.1 copy.20
  15.8 0.1 reshape.284
  15.9 0.1 copy.19
  16.0 0.1 reshape.276
  16.1 0.1 copy.25
  16.2 0.1 reshape.324
  16.3 0.1 copy.26
  16.4 0.1 reshape.332
  16.5 2.4 scatter_custom_fusion
  18.9 3.8 %copy_multiply_fusion = bf16[4,8,3,128,128]{4,3,2,0,1:T(8,128)(2,1)} fusion(bf16[4,8,3,128,128]{4,3,2,1,0:T(8,128)(2,1)} %param.8, bf16[4,8,3]{2,0,1:T(4,128)(2,1)S(1)} %fusion.9), kind=kLoop, calls=%fused_computation.11 | loop fusion | flops 1572864 | bytes 6291648 | tf_op jit(solution)/shard_map/mul | solution.py:23
  22.8 207.5 %all-reduce.3.cloned.1.call-done = (bf16[4,128,768]{2,1,0:T(8,128)(2,1)}, bf16[4,128,768]{2,1,0:T(8,128)(2,1)}, bf16[4,128,768]{2,1,0:T(8,128)(2,1)}, bf16[4,128...) async-done(((bf16[4,128,768]{2,1,0:T(8,128)(2,1)}, ...) | async-done | bytes 6291472 | tf_op jit(solution)/shard_map/psum | solution.py:9
  230.2 1.8 gather_fusion.6
  232.1 2.7 fusion.2
  234.8 1.8 gather_fusion.5
  236.6 3.4 %gather_fusion.4 = bf16[12,128,768]{2,1,0:T(8,128)(2,1)} fusion(bf16[4,128,768]{2,1,0:T(8,128)(2,1)} %get-tuple-element.16, s32[1024]{0:T(1024)S(1)} %pad_clamp_fusion.5), kind=kCustom, calls=%fused_computation.4 | custom fusion | bytes 4718640 | tf_op jit(solution)/shard_map/gather | solution.py:29
  240.0 3.3 %gather_fusion.3 = bf16[12,128,768]{2,1,0:T(8,128)(2,1)} fusion(bf16[4,128,768]{2,1,0:T(8,128)(2,1)} %get-tuple-element.17, s32[1024]{0:T(1024)S(1)} %pad_clamp_fusion.6), kind=kCustom, calls=%fused_computation.3 | custom fusion | bytes 4718640 | tf_op jit(solution)/shard_map/gather | solution.py:29
  243.3 3.4 %gather_fusion.2 = bf16[12,128,768]{2,1,0:T(8,128)(2,1)} fusion(bf16[4,128,768]{2,1,0:T(8,128)(2,1)} %get-tuple-element.18, s32[1024]{0:T(1024)S(1)} %pad_clamp_fusion.7), kind=kCustom, calls=%fused_computation.2 | custom fusion | bytes 4718640 | tf_op jit(solution)/shard_map/gather | solution.py:29
  246.7 3.3 %gather_fusion.1 = bf16[12,128,768]{2,1,0:T(8,128)(2,1)} fusion(bf16[4,128,768]{2,1,0:T(8,128)(2,1)} %get-tuple-element.19, s32[1024]{0:T(1024)S(1)} %pad_clamp_fusion.8), kind=kCustom, calls=%fused_computation.1 | custom fusion | bytes 4718640 | tf_op jit(solution)/shard_map/gather | solution.py:29
  250.0 3.3 %gather_fusion.7 = bf16[12,128,768]{2,1,0:T(8,128)(2,1)} fusion(bf16[4,128,768]{2,1,0:T(8,128)(2,1)} %get-tuple-element.13, s32[1024]{0:T(1024)S(1)} %pad_clamp_fusion.2), kind=kCustom, calls=%fused_computation.7 | custom fusion | bytes 4718640 | tf_op jit(solution)/shard_map/gather | solution.py:29
  253.3 3.3 %gather_fusion.8 = bf16[12,128,768]{2,1,0:T(8,128)(2,1)} fusion(bf16[4,128,768]{2,1,0:T(8,128)(2,1)} %get-tuple-element.20, s32[1024]{0:T(1024)S(1)} %pad_clamp_fusion.1), kind=kCustom, calls=%fused_computation.8 | custom fusion | bytes 4718640 | tf_op jit(solution)/shard_map/gather | solution.py:29
  256.6 1.7 fusion.3
  258.3 0.0 copy-start.2
  258.3 0.3 copy-done.1
  258.6 2.4 fusion.4
  261.0 0.0 copy-start.3
  261.0 0.0 copy-done.2
  261.0 0.6 fusion.5
  261.6 1.1 copy-done.3
  262.6 0.6 fusion.6
  263.2 0.3 copy-done.4
  263.5 0.6 fusion.7
  264.1 0.9 copy-done.5
  265.0 0.6 fusion.1
  265.5 0.4 copy-done.6
  265.9 0.5 copy-done.7
  266.4 0.9 bitcast_add_fusion
  267.3 2.6 gather_fusion.9
  269.9 0.0 reduce-scatter.2.cloned.1.call-update
  269.9 0.0 all-gather.2.cloned.1.call-done
  270.0 40.2 %reduce-scatter.2.cloned.1.call-done = f32[64,768]{1,0:T(8,128)} async-done(((f32[512,768]{1,0:T(8,128)}), f32[64,768]{1,0:T(8,128)}) %reduce-scatter.2.cloned.1.call-update) | async-done | bytes 196624 | tf_op jit(solution)/shard_map/reduce_scatter | solution.py:37
  310.1 2.6 fusion
  (23 shorter events, 0.1 us)
Async XLA Ops:
  7.4 1.1 copy-start
  7.4 222.8 %all-reduce.3.cloned.1.call-start = ((), (), s32[]{:S(2)}) async-start(), calls=%async_computation.3 | async-start | bytes 12582912 | tf_op jit(solution)/shard_map/psum | solution.py:9
  13.5 0.7 copy-start.8
  13.5 1.5 copy-start.9
  13.5 256.4 %all-gather.2.cloned.1.call-start = ((), (), s32[]{:S(2)}) async-start(), calls=%async_computation.2 | async-start | bytes 1769472 | tf_op jit(solution)/shard_map/all_gather | solution.py:38
  14.1 296.0 %reduce-scatter.2.cloned.1.call-start = ((), (), s32[]{:S(2)}) async-start(), calls=%async_computation.1 | async-start | bytes 1769472 | tf_op jit(solution)/shard_map/reduce_scatter | solution.py:37
  256.6 2.0 copy-start.1
  258.3 2.7 copy-start.2
  261.0 1.7 copy-start.3
  261.6 1.9 copy-start.4
  263.2 1.7 copy-start.5
  264.1 1.8 copy-start.6
  264.1 2.3 copy-start.7
Sparse Core Ops, SparseCore 0:
  13.6 216.5 all-reduce.2
Sparse Core Ops, SparseCore 1:
  16.0 48.5 all-gather.1
  270.0 40.1 reduce-scatter.1
where the time goes:
time: 324 us; the launch traced here: 320 us
  waiting for transfers between devices  248 us (77%)
  local copies, waits for them, and re-layouts  36.5 us (11%)
  between operations  15.1 us (5%)
  matrix products  12.5 us (4%)
  other arithmetic  7.71 us (2%)
    psum x1, waiting for transfers between devices, broadcast(): return lax.psum(jnp.where(mine, x, jnp.zeros_like(x)), axis)  207 us
    reduce_scatter x1, waiting for transfers between devices, shards(): lax.psum_scatter(partial_orig, 'rep', scatter_dimension=0, tiled=True)  40.2 us
    gather x8, local copies, waits for them, and re-layouts, shards(): chosen = pieces[adj_cols[:, section]]  23.6 us
    dot_general x8, matrix products, shards(): jnp.einsum('rkij,rkjd->rid', masked[:, section], chosen, preferred_elemen...  9.97 us
  transfers between devices with their start and end apart: 3, of which 2 were waited for; matrix products, arithmetic and copies ran while one was open for 14% of the time, Pallas kernels for 0%

commit v1 on v0

v1 whole, which is shorter than its diff:
```python
import functools

import jax
import jax.numpy as jnp
from jax import lax
from jax.experimental import pallas as pl
from jax.experimental.pallas import tpu as pltpu
from jax.sharding import PartitionSpec as P

MESH = pl.DeviceIdType.MESH
NY, NX, NC, NZ = 8, 4, 2, 8
BLK = 128
RB = 4
KB = 3
SLAB = RB * BLK
CHUNKS = 6
STEPS = CHUNKS * RB
LAG_X1 = 4
LAG_X2 = 8
LAG_COMPUTE = 12
LAG_WEIGHT = 14
LAG_FINAL = 24
ITERS = 4 * (CHUNKS - 1) + LAG_FINAL + 1
YP1, YM1, YP2, YM2, XP, XM, FR, FL, SIB = range(9)
KINDS = SIB + NX


def kernel(
    feat_hbm, order_ref, adj_hbm, cols_ref, count_ref, w_hbm, out_ref,
    slabs, adj, raw, dense, feat, perm, w_own, w_all, part, z_out, z_in, total,
    load_sem, send_sem, recv_sem, sib_sem, z_send, z_recv, w_send, w_recv, w_sib_send, w_sib_recv,
):
    row = lax.axis_index("row")
    rep = lax.axis_index("rep")
    c = row % NC
    x = (row // NC) % NX
    y = row // (NC * NX)
    d = (y - rep + NY) % NY

    def device(dy, dx, dc):
        return ((((y + dy) % NY) * NX + (x + dx) % NX) * NC + (c + dc) % NC, rep)

    left, right, sibling = device(0, NX - 1, 0), device(0, 1, 0), device(0, 0, 1)
    up1, down1, up2, down2 = device(1, 0, 0), device(NY - 1, 0, 0), device(2, 0, 0), device(NY - 2, 0, 0)

    barrier = pltpu.get_barrier_semaphore()
    for near in (left, right, sibling, up1, down1, up2, down2):
        pl.semaphore_signal(barrier, inc=1, device_id=near, device_id_type=MESH)
    for k in range(1, NZ):
        pl.semaphore_signal(barrier, inc=1, device_id=(row, (rep + k) % NZ), device_id_type=MESH)

    load_feat = pltpu.make_async_copy(feat_hbm, feat, load_sem.at[0])
    load_w = pltpu.make_async_copy(w_hbm, w_own, load_sem.at[1])
    load_adj = pltpu.make_async_copy(adj_hbm, adj.at[pl.ds(0, RB * NZ * KB)], load_sem.at[2])

    @pl.when(d == 0)
    def _():
        load_feat.start()

    load_w.start()
    load_adj.start()

    local = order_ref[...] - row * SLAB
    rows_of = lax.broadcasted_iota(jnp.int32, (SLAB, SLAB), 0)
    perm[...] = (rows_of == local).astype(jnp.float32).astype(jnp.bfloat16)
    adj[RB * NZ * KB] = jnp.zeros((BLK, BLK), jnp.bfloat16)
    total[...] = jnp.zeros_like(total)

    def unit(s, x0):
        return slabs.at[s // RB, c * NX + x0, pl.ds((s % RB) * BLK, BLK)]

    @pl.when(d == 0)
    def _():
        load_feat.wait()
        ordered = lax.dot_general(
            perm[...], feat[...], (((0,), (0,)), ((), ())), preferred_element_type=jnp.float32
        ).astype(jnp.bfloat16)
        for ch in range(CHUNKS):
            slabs[ch, c * NX + x] = ordered[:, ch * BLK:(ch + 1) * BLK]

    load_w.wait()
    half = CHUNKS // 2
    w_all[pl.ds(c * half, half), :, pl.ds(pl.multiple_of(rep * BLK, BLK), BLK)] = w_own[pl.ds(c * half, half)]
    pl.semaphore_wait(barrier, 7 + NZ - 1)

    def copy_to(s, x0, kind, target):
        ref = unit(s, x0)
        return pltpu.make_async_remote_copy(
            src_ref=ref, dst_ref=ref, send_sem=send_sem.at[kind, s], recv_sem=recv_sem.at[s, x0],
            device_id=target, device_id_type=MESH,
        )

    def copy_sib(s, x0, rel):
        ref = unit(s, x0)
        return pltpu.make_async_remote_copy(
            src_ref=ref, dst_ref=ref, send_sem=send_sem.at[SIB + rel, s], recv_sem=sib_sem.at[s // RB],
            device_id=sibling, device_id_type=MESH,
        )

    def y_sends(s):
        even = s % 2 == 0
        return (
            ((d == 0) | ((d == 2) & even), YP2, up2),
            ((d == 0) | ((d == NY - 2) & jnp.logical_not(even)), YM2, down2),
            ((d == 2) | (d == NY - 2), YP1, up1),
            ((d == 2) | (d == NY - 2), YM1, down1),
        )

    def w_copy(k):
        return pltpu.make_async_remote_copy(
            src_ref=w_own.at[pl.ds(c * half, half)],
            dst_ref=w_all.at[pl.ds(c * half, half), :, pl.ds(pl.multiple_of(rep * BLK, BLK), BLK)],
            send_sem=w_send.at[k - 1], recv_sem=w_recv,
            device_id=(row, (rep + k) % NZ), device_id_type=MESH,
        )

    def w_sib_copy():
        ref = w_all.at[pl.ds(c * half, half)]
        return pltpu.make_async_remote_copy(
            src_ref=ref, dst_ref=ref, send_sem=w_sib_send, recv_sem=w_sib_recv,
            device_id=sibling, device_id_type=MESH,
        )

    def z_copy(ch, k):
        peer = (rep + k) % NZ
        return pltpu.make_async_remote_copy(
            src_ref=z_out.at[ch, peer], dst_ref=z_in.at[ch, rep],
            send_sem=z_send.at[k - 1, ch], recv_sem=z_recv.at[ch],
            device_id=(row, peer), device_id_type=MESH,
        )

    Z_ORDER = (4, 3, 5, 2, 6, 1, 7)
    for k in Z_ORDER:
        w_copy(k).start()

    def iteration(i, carry):
        @pl.when(i < STEPS)
        def _():
            s = i

            @pl.when(d != 0)
            def _():
                copy_to(s, x, XP, right).wait_recv()

            for cond, kind, target in y_sends(s):
                @pl.when(cond)
                def _(kind=kind, target=target):
                    copy_to(s, x, kind, target).start()

            copy_to(s, x, XP, right).start()
            copy_to(s, x, XM, left).start()
            copy_sib(s, x, 0).start()

        @pl.when((i >= LAG_X1) & (i < STEPS + LAG_X1))
        def _():
            s = i - LAG_X1
            xl, xr = (x + NX - 1) % NX, (x + 1) % NX
            copy_to(s, xl, FR, right).wait_recv()

            @pl.when(s % 2 == 0)
            def _():
                copy_to(s, xl, FR, right).start()

            copy_sib(s, xl, 1).start()
            copy_to(s, xr, FL, left).wait_recv()

            @pl.when(s % 2 == 1)
            def _():
                copy_to(s, xr, FL, left).start()

            copy_sib(s, xr, 3).start()

        @pl.when((i >= LAG_X2) & (i < STEPS + LAG_X2))
        def _():
            s = i - LAG_X2
            xo = (x + 2) % NX
            copy_to(s, xo, FR, right).wait_recv()
            copy_sib(s, xo, 2).start()

        @pl.when(i == 0)
        def _():
            load_adj.wait()

        @pl.when(i < 2 * NX)
        def _():
            jj = i
            j = (jj % NX) * NC + jj // NX
            for b in range(RB):
                cols = [cols_ref[k, b, j] for k in range(KB)]
                n = count_ref[b, j]
                base = (b * NZ + j) * KB
                for cb in range(RB):
                    index = jnp.int32(RB * NZ * KB)
                    for k in range(KB):
                        index = jnp.where((n > k) & (cols[k] == cb), base + k, index)
                    raw[b * BLK:(b + 1) * BLK, cb * BLK:(cb + 1) * BLK] = adj[index]
            dense[jj] = jnp.dot(
                perm[...], raw[...], preferred_element_type=jnp.float32
            ).astype(jnp.bfloat16)

        at = i - LAG_COMPUTE

        @pl.when((at >= 0) & (at < STEPS))
        def _():
            ch = at // RB
            q = at % RB

            @pl.when(q == 2)
            def _():
                ref = slabs.at[ch, pl.ds((1 - c) * NX, NX)]
                pltpu.make_async_remote_copy(
                    src_ref=ref, dst_ref=ref, send_sem=send_sem.at[SIB, 0], recv_sem=sib_sem.at[ch],
                    device_id=sibling, device_id_type=MESH,
                ).wait_recv()

            layer = jnp.where(q < 2, c, 1 - c)
            first = layer * NX + (q % 2) * 2
            update = jnp.dot(dense[first], slabs[ch, first], preferred_element_type=jnp.float32) + jnp.dot(
                dense[first + 1], slabs[ch, first + 1], preferred_element_type=jnp.float32
            )

            @pl.when(q == 0)
            def _():
                part[...] = update

            @pl.when(q > 0)
            def _():
                part[...] += update

            @pl.when(q == RB - 1)
            def _():
                z_out[ch] = part[...].astype(jnp.bfloat16).reshape(NZ, SLAB // NZ, BLK)
                for k in Z_ORDER:
                    z_copy(ch, k).start()
                z_in[ch, rep] = z_out[ch, rep]

        @pl.when(i == LAG_WEIGHT)
        def _():
            ref = w_all.at[pl.ds(c * half, half), :, pl.ds(0, (NZ - 1) * BLK)]
            pltpu.make_async_remote_copy(
                src_ref=ref, dst_ref=ref, send_sem=w_sib_send, recv_sem=w_recv,
                device_id=sibling, device_id_type=MESH,
            ).wait_recv()
            w_sib_copy().start()

        @pl.when(i == LAG_FINAL - 1)
        def _():
            ref = w_all.at[pl.ds((1 - c) * half, half)]
            pltpu.make_async_remote_copy(
                src_ref=ref, dst_ref=ref, send_sem=w_sib_send, recv_sem=w_sib_recv,
                device_id=sibling, device_id_type=MESH,
            ).wait_recv()

        last = i - LAG_FINAL

        @pl.when((last >= 0) & (last % RB == 0))
        def _():
            ch = last // RB

            @pl.when(ch == CHUNKS - 1)
            def _():
                def sent(s, carry):
                    for cond, kind, target in y_sends(s):
                        @pl.when(cond)
                        def _(kind=kind, target=target):
                            copy_to(s, x, kind, target).wait_send()
                    copy_to(s, x, XP, right).wait_send()
                    copy_to(s, x, XM, left).wait_send()

                    @pl.when(s % 2 == 0)
                    def _():
                        copy_to(s, (x + NX - 1) % NX, FR, right).wait_send()

                    @pl.when(s % 2 == 1)
                    def _():
                        copy_to(s, (x + 1) % NX, FL, left).wait_send()

                    for rel in range(NX):
                        copy_sib(s, x, rel).wait_send()
                    return carry

                lax.fori_loop(0, STEPS, sent, 0)
                w_sib_copy().wait_send()
                for k in Z_ORDER:
                    w_copy(k).wait_send()

            ref = z_in.at[ch, pl.ds(0, NZ - 1)]
            pltpu.make_async_remote_copy(
                src_ref=ref, dst_ref=ref, send_sem=w_sib_send, recv_sem=z_recv.at[ch],
                device_id=sibling, device_id_type=MESH,
            ).wait_recv()
            rounded = jnp.sum(z_in[ch].astype(jnp.float32), axis=0).astype(jnp.bfloat16)
            total[...] += jnp.dot(rounded, w_all[ch], preferred_element_type=jnp.float32)

        return carry

    lax.fori_loop(0, ITERS, iteration, 0)
    out_ref[...] = jnp.maximum(total[...], 0.0).astype(jnp.bfloat16)

    def z_sent(ch, carry):
        for k in Z_ORDER:
            z_copy(ch, k).wait_send()
        return carry

    lax.fori_loop(0, CHUNKS, z_sent, 0)


def shards(features, order, adj_values, adj_cols, adj_count, weight):
    hid = NZ * BLK
    bf16, f32 = jnp.bfloat16, jnp.float32
    dma = pltpu.SemaphoreType.DMA
    any_space = pl.BlockSpec(memory_space=pl.ANY)
    return pl.pallas_call(
        kernel,
        out_shape=jax.ShapeDtypeStruct((SLAB // NZ, hid), bf16),
        in_specs=[
            any_space,
            pl.BlockSpec(memory_space=pltpu.VMEM),
            any_space,
            pl.BlockSpec(memory_space=pltpu.SMEM),
            pl.BlockSpec(memory_space=pltpu.SMEM),
            any_space,
        ],
        out_specs=pl.BlockSpec(memory_space=pltpu.VMEM),
        scratch_shapes=[
            pltpu.VMEM((CHUNKS, NC * NX, SLAB, BLK), bf16),
            pltpu.VMEM((RB * NZ * KB + 1, BLK, BLK), bf16),
            pltpu.VMEM((SLAB, SLAB), bf16),
            pltpu.VMEM((NC * NX, SLAB, SLAB), bf16),
            pltpu.VMEM((SLAB, CHUNKS * BLK), bf16),
            pltpu.VMEM((SLAB, SLAB), bf16),
            pltpu.VMEM((CHUNKS, BLK, BLK), bf16),
            pltpu.VMEM((CHUNKS, BLK, hid), bf16),
            pltpu.VMEM((SLAB, BLK), f32),
            pltpu.VMEM((CHUNKS, NZ, SLAB // NZ, BLK), bf16),
            pltpu.VMEM((CHUNKS, NZ, SLAB // NZ, BLK), bf16),
            pltpu.VMEM((SLAB // NZ, hid), f32),
            dma((3,)),
            dma((KINDS, STEPS)),
            dma((STEPS, NX)),
            dma((CHUNKS,)),
            dma((NZ - 1, CHUNKS)),
            dma((CHUNKS,)),
            dma((NZ - 1,)),
            dma,
            dma,
            dma,
        ],
        compiler_params=pltpu.CompilerParams(
            collective_id=0, has_side_effects=True, vmem_limit_bytes=56 << 20
        ),
    )(
        features,
        order.reshape(1, SLAB),
        adj_values.reshape(RB * NZ * KB, BLK, BLK),
        adj_cols.transpose(2, 0, 1),
        adj_count,
        weight.reshape(CHUNKS, BLK, BLK),
    )


def solution(mesh):
    placed = (
        P("row", None),
        P("row"),
        P("row", "rep", None, None, None),
        P("row", "rep", None),
        P("row", "rep"),
        P(None, "rep"),
    )
    return jax.shard_map(
        shards, mesh=mesh, in_specs=placed, out_specs=P(("row", "rep"), None), check_vma=False
    )
```

time: 324 us -> 71.8 us (0.22); the launches traced: 320 us -> 71.6 us
  waiting for transfers between devices: 248 us -> 0 us
  Pallas kernels: 0 us -> 70.1 us
  local copies, waits for them, and re-layouts: 36.5 us -> 1.57 us
  between operations: 15.1 us -> 0.01 us
  matrix products: 12.5 us -> 0 us
  other arithmetic: 7.71 us -> 0 us
    psum x1 -> x0, waiting for transfers between devices: 207 us -> none  [broadcast(): return lax.psum(jnp.where(mine, x, jnp.zeros_like(x)), axis)]
    pallas_call x0 -> x1, Pallas kernels: none -> 70.1 us  [shards(): pl.pallas_call(kernel, out_shape=jax.ShapeDtypeStruct((SLAB // NZ, hid),...]
    reduce_scatter x1 -> x0, waiting for transfers between devices: 40.2 us -> none  [shards(): lax.psum_scatter(partial_orig, 'rep', scatter_dimension=0, tiled=True)]
    gather x10 -> x0, local copies, waits for them, and re-layouts: 28.3 us -> none  [the longest x8 23.6 us: shards(): chosen = pieces[adj_cols[:, section]]]
    dot_general x9 -> x0, matrix products: 12.5 us -> none  [the longest x8 9.97 us: shards(): jnp.einsum('rkij,rkjd->rid', masked[:, section], chosen, preferred_elemen...]
    mul x1 -> x0, other arithmetic: 3.83 us -> none  [shards(): masked = adj_values * live_slots[:, :, :, None, None]]
    select_n x7 -> x0, other arithmetic: 3.72 us -> none  [the longest x1 2.93 us: broadcast(): return lax.psum(jnp.where(mine, x, jnp.zeros_like(x)), axis)]
  transfers between devices with their start and end apart: 3 -> 0, of which waited for: 2 -> 0; matrix products, arithmetic and copies ran while one was open for 14% -> 0% of each run, Pallas kernels for 0% -> 0%
where the time goes in v1:
time: 71.8 us; the launch traced here: 71.6 us
  Pallas kernels  70.1 us (98%)
  local copies, waits for them, and re-layouts  1.57 us (2%)
    pallas_call x1, Pallas kernels, shards(): pl.pallas_call(kernel, out_shape=jax.ShapeDtypeStruct((SLAB // NZ, hid),...  70.1 us
    unnamed x1, local copies, waits for them, and re-layouts  1.57 us

profile of v1, /device:TPU:1, one launch (start us, length us, event | category | flops | bytes accessed | tf_op | source)
XLA Modules:
  0.0 71.6 jit_solution(5665536843952791394)
XLA Ops:
  0.0 70.1 %shard_map.64 = bf16[64,1024]{1,0:T(8,128)(2,1)} custom-call(bf16[512,768]{1,0:T(8,128)(2,1)} %feat_hbm.1, s32[1,512]{1,0:T(1,128)} %bitcast.7, bf16[96,128,128]{2,1,0:T(8,128)(2,1)} %bitcast.4, s32[3,4,8]{2,1,0:T(4,128)} %bitcast.6, s32[4,8]{1,0:T(4,128)} %count_ref.1, bf16[6,128,128]{2,1,0:T(8,128)(2,1)} %bitcast.5), custom_call_target="tpu_custom_call" | custom-call | tf_op jit(solution)/shard_map/pallas_call | solution.py:313
  70.1 1.6 %copy.8 = bf16[64,1024]{1,0:T(8,128)(2,1)} copy(bf16[64,1024]{1,0:T(8,128)(2,1)} %shard_map.64) | data formatting | bytes 262144

commit v2 on v0

v2 whole, which is shorter than its diff:
```python
import functools

import jax
import jax.numpy as jnp
from jax import lax
from jax.experimental import pallas as pl
from jax.experimental.pallas import tpu as pltpu
from jax.sharding import PartitionSpec as P

MESH = pl.DeviceIdType.MESH
NY, NX, NC, NZ = 8, 4, 2, 8
BLK = 128
RB = 4
KB = 3
SLAB = RB * BLK
CHUNKS = 6
SUB = 4
ROWS = SLAB // SUB
STEPS = CHUNKS * SUB
PRE = 6
LAG_X1 = 4
LAG_X2 = 8
LAG_COMPUTE = 12
ITERS = LAG_X2 + STEPS
DIRECT = STEPS - SUB
READY_AT = 4
WEIGHT_AT = 22
YP1, YM1, YP2, YM2, XP, XM, XO, FR, FL, SIB = range(10)
KINDS = SIB + 1


def kernel(
    feat_hbm, order_hbm, adj_hbm, cols_hbm, count_hbm, w_hbm, out_ref,
    slabs, adj, dense, feat, perm, order, cols_ref, count_ref, w_all, part, z_out, z_in, total,
    load_sem, send_sem, recv_sem, sib_sem, z_send, z_recv, w_send, w_recv, w_sib_send, w_sib_recv, ready,
):
    row = lax.axis_index("row")
    rep = lax.axis_index("rep")
    c = row % NC
    x = (row // NC) % NX
    y = row // (NC * NX)
    d = (y - rep + NY) % NY

    def device(dy, dx, dc):
        return ((((y + dy) % NY) * NX + (x + dx) % NX) * NC + (c + dc) % NC, rep)

    left, right, opposite, sibling = device(0, NX - 1, 0), device(0, 1, 0), device(0, 2, 0), device(0, 0, 1)
    up1, down1, up2, down2 = device(1, 0, 0), device(NY - 1, 0, 0), device(2, 0, 0), device(NY - 2, 0, 0)

    barrier = pltpu.get_barrier_semaphore()
    near = (left, right, opposite, sibling, up1, down1, up2, down2)
    for other in near:
        pl.semaphore_signal(barrier, inc=1, device_id=other, device_id_type=MESH)
    for k in range(1, NZ):
        @pl.when(rep + k < NZ)
        def _(k=k):
            pl.semaphore_signal(barrier, inc=1, device_id=(row, rep + k), device_id_type=MESH)

    load_order = pltpu.make_async_copy(order_hbm, order, load_sem.at[0])
    load_feat = pltpu.make_async_copy(feat_hbm, feat, load_sem.at[1])
    load_adj = pltpu.make_async_copy(adj_hbm, adj.at[pl.ds(0, RB * NZ * KB)], load_sem.at[2])
    load_cols = pltpu.make_async_copy(cols_hbm, cols_ref, load_sem.at[3])
    load_count = pltpu.make_async_copy(count_hbm, count_ref, load_sem.at[4])
    load_w = pltpu.make_async_copy(w_hbm, w_all.at[rep], load_sem.at[5])
    load_order.start()

    @pl.when(d == 0)
    def _():
        load_feat.start()

    load_adj.start()
    load_cols.start()
    load_count.start()
    load_w.start()
    load_order.wait()
    local = order[...] - row * SLAB
    rows_of = lax.broadcasted_iota(jnp.int32, (SLAB, SLAB), 0)
    perm[...] = (rows_of == local).astype(jnp.float32).astype(jnp.bfloat16)

    def unit(s, x0):
        return slabs.at[s // SUB, c * NX + x0, pl.ds((s % SUB) * ROWS, ROWS)]

    @pl.when(d == 0)
    def _():
        load_feat.wait()
        ordered = lax.dot_general(
            perm[...], feat[...], (((0,), (0,)), ((), ())), preferred_element_type=jnp.float32
        ).astype(jnp.bfloat16)
        for ch in range(CHUNKS):
            slabs[ch, c * NX + x] = ordered[:, ch * BLK:(ch + 1) * BLK]

    pl.semaphore_wait(barrier, len(near) + rep)
    for k in range(1, NZ):
        @pl.when(rep >= k)
        def _(k=k):
            pl.semaphore_signal(ready, inc=1, device_id=(row, rep - k), device_id_type=MESH)

    def remote(src, dst, sent, landed, target):
        return pltpu.make_async_remote_copy(
            src_ref=src, dst_ref=dst, send_sem=sent, recv_sem=landed, device_id=target, device_id_type=MESH
        )

    def copy_to(s, x0, kind, target):
        return remote(unit(s, x0), unit(s, x0), send_sem.at[kind], recv_sem.at[s, x0], target)

    def copy_sib(s, x0):
        return remote(unit(s, x0), unit(s, x0), send_sem.at[SIB], sib_sem.at[s // SUB], sibling)

    second = (d == 2) | (d == NY - 2)

    half = CHUNKS // 2
    mine = pl.ds(c * half, half)

    def w_copy(k):
        ref = w_all.at[rep, mine]
        return remote(ref, ref, w_send, w_recv, (row, (rep + k) % NZ))

    def w_sib():
        ref = w_all.at[:, mine]
        return remote(ref, ref, w_sib_send, w_sib_recv, sibling)

    load_w.wait()
    for k in (4, 3, 5, 2, 6, 1, 7):
        pl.when(rep + k >= NZ)(w_copy(k).start)

    def own_step(s):
        even = s % 2 == 0
        for cond, kind, target in (
            ((d == 0) | ((d == 2) & even), YP2, up2),
            ((d == 0) | ((d == NY - 2) & jnp.logical_not(even)), YM2, down2),
            (second, YP1, up1),
            (second, YM1, down1),
        ):
            pl.when(cond)(copy_to(s, x, kind, target).start)
        copy_to(s, x, XP, right).start()
        copy_to(s, x, XM, left).start()
        pl.when(s >= DIRECT)(copy_to(s, x, XO, opposite).start)
        copy_sib(s, x).start()

    def arrive(s, x0):
        copy_to(s, x0, XP, right).wait_recv()

    def all_sent(kind, chunks):
        ref = slabs.at[pl.ds(0, chunks), 0]
        remote(ref, ref, send_sem.at[kind], w_recv, right).wait_send()

    def z_copy(ch, peer):
        return remote(z_out.at[ch, peer], z_in.at[ch, rep], z_send, z_recv.at[ch], (row, peer))

    @pl.when(d == 0)
    def _():
        def first(s, carry):
            own_step(s)
            return carry

        lax.fori_loop(0, PRE, first, 0)

    adj[RB * NZ * KB] = jnp.zeros((BLK, BLK), jnp.bfloat16)
    load_cols.wait()
    load_count.wait()
    load_adj.wait()

    def build(jj, carry):
        j = (jj % NX) * NC + jj // NX
        for b in range(RB):
            cols = [cols_ref[k, b, j] for k in range(KB)]
            n = count_ref[b, j]
            base = (b * NZ + j) * KB
            for cb in range(RB):
                index = jnp.int32(RB * NZ * KB)
                for k in range(KB):
                    index = jnp.where((n > k) & (cols[k] == cb), base + k, index)
                dense[jj, b * BLK:(b + 1) * BLK, cb * BLK:(cb + 1) * BLK] = adj[index]
        return carry

    lax.fori_loop(0, NC * NX, build, 0)
    total[...] = jnp.zeros_like(total)

    def product(m, carry):
        ch, q = m // RB, m % RB

        @pl.when(q == 2)
        def _():
            ref = slabs.at[ch, pl.ds((1 - c) * NX, NX)]
            remote(ref, ref, w_sib_send, sib_sem.at[ch], sibling).wait_recv()

        layer = jnp.where(q < 2, c, 1 - c)
        first = layer * NX + (q % 2) * 2
        update = jnp.dot(dense[first], slabs[ch, first], preferred_element_type=jnp.float32) + jnp.dot(
            dense[first + 1], slabs[ch, first + 1], preferred_element_type=jnp.float32
        )

        @pl.when(q == 0)
        def _():
            part[...] = update

        @pl.when(q > 0)
        def _():
            part[...] += update

        @pl.when(q == RB - 1)
        def _():
            initial = jnp.dot(perm[...], part[...].astype(jnp.bfloat16), preferred_element_type=jnp.float32)
            z_out[ch] = initial.astype(jnp.bfloat16).reshape(NZ, SLAB // NZ, BLK)
            for peer in range(NZ):
                pl.when(rep != peer)(z_copy(ch, peer).start)
            z_in[ch, rep] = z_out[ch, rep]

        return carry

    def iteration(i, carry):
        now = i + jnp.where(d == 0, PRE, 0)

        @pl.when((d != 0) & (i < STEPS))
        def _():
            arrive(i, x)

        @pl.when(now < STEPS)
        def _():
            own_step(now)

        @pl.when((i >= LAG_X1) & (i < STEPS + LAG_X1))
        def _():
            s = i - LAG_X1
            forward = s < DIRECT
            to_right = s % 2 == 0
            from_left, from_right = (x + NX - 1) % NX, (x + 1) % NX
            arrive(s, from_left)
            pl.when(forward & to_right)(copy_to(s, from_left, FR, right).start)
            copy_sib(s, from_left).start()
            arrive(s, from_right)
            pl.when(forward & jnp.logical_not(to_right))(copy_to(s, from_right, FL, left).start)
            copy_sib(s, from_right).start()

        @pl.when(i >= LAG_X2)
        def _():
            arrive(i - LAG_X2, (x + 2) % NX)
            copy_sib(i - LAG_X2, (x + 2) % NX).start()

        @pl.when(i == READY_AT)
        def _():
            @pl.when(rep < NZ - 1)
            def _():
                pl.semaphore_wait(ready, NZ - 1 - rep)

            for k in (4, 3, 5, 2, 6, 1, 7):
                pl.when(rep + k < NZ)(w_copy(k).start)

        @pl.when(i == WEIGHT_AT)
        def _():
            ref = w_all.at[pl.ds(0, NZ - 1), mine]
            remote(ref, ref, w_send, w_recv, sibling).wait()
            w_sib().start()

        @pl.when((i >= LAG_COMPUTE) & (i < LAG_COMPUTE + (CHUNKS - 1) * SUB))
        def _():
            at = (i - LAG_COMPUTE) * (RB // SUB)
            lax.fori_loop(at, at + RB // SUB, product, 0)

        return carry

    lax.fori_loop(0, ITERS, iteration, 0)
    lax.fori_loop((CHUNKS - 1) * RB, CHUNKS * RB, product, 0)

    for kind in (XP, XM):
        all_sent(kind, CHUNKS)
    all_sent(XO, 1)
    for kind in (FR, FL):
        ref = slabs.at[0, pl.ds(0, CHUNKS - 1), pl.ds(0, SLAB // 2)]
        remote(ref, ref, send_sem.at[kind], w_recv, right).wait_send()
    ref = slabs.at[:, pl.ds(0, NX)]
    remote(ref, ref, send_sem.at[SIB], w_recv, right).wait_send()

    @pl.when(d == 0)
    def _():
        all_sent(YP2, CHUNKS)
        all_sent(YM2, CHUNKS)

    @pl.when(second)
    def _():
        all_sent(YP1, CHUNKS)
        all_sent(YM1, CHUNKS)

    pl.when(d == 2)(functools.partial(all_sent, YP2, CHUNKS // 2))
    pl.when(d == NY - 2)(functools.partial(all_sent, YM2, CHUNKS // 2))
    w_sib().wait()

    def finish(ch, carry):
        ref = z_in.at[ch, pl.ds(0, NZ - 1)]
        remote(ref, ref, w_sib_send, z_recv.at[ch], sibling).wait_recv()
        rounded = jnp.sum(z_in[ch].astype(jnp.float32), axis=0).astype(jnp.bfloat16)
        for k in range(NZ):
            total[:, k * BLK:(k + 1) * BLK] += jnp.dot(rounded, w_all[k, ch], preferred_element_type=jnp.float32)
        return carry

    lax.fori_loop(0, CHUNKS, finish, 0)
    out_ref[...] = jnp.maximum(total[...], 0.0).astype(jnp.bfloat16)
    ref = z_out.at[:, pl.ds(0, NZ - 1)]
    remote(ref, ref, z_send, w_sib_recv, sibling).wait_send()


def shards(features, order, adj_values, adj_cols, adj_count, weight):
    hid = NZ * BLK
    bf16, f32, i32 = jnp.bfloat16, jnp.float32, jnp.int32
    dma = pltpu.SemaphoreType.DMA
    return pl.pallas_call(
        kernel,
        out_shape=jax.ShapeDtypeStruct((SLAB // NZ, hid), bf16),
        in_specs=[pl.BlockSpec(memory_space=pl.ANY)] * 6,
        out_specs=pl.BlockSpec(memory_space=pltpu.VMEM),
        scratch_shapes=[
            pltpu.VMEM((CHUNKS, NC * NX, SLAB, BLK), bf16),
            pltpu.VMEM((RB * NZ * KB + 1, BLK, BLK), bf16),
            pltpu.VMEM((NC * NX, SLAB, SLAB), bf16),
            pltpu.VMEM((SLAB, CHUNKS * BLK), bf16),
            pltpu.VMEM((SLAB, SLAB), bf16),
            pltpu.VMEM((1, SLAB), i32),
            pltpu.SMEM((KB, RB, NZ), i32),
            pltpu.SMEM((RB, NZ), i32),
            pltpu.VMEM((NZ, CHUNKS, BLK, BLK), bf16),
            pltpu.VMEM((SLAB, BLK), f32),
            pltpu.VMEM((CHUNKS, NZ, SLAB // NZ, BLK), bf16),
            pltpu.VMEM((CHUNKS, NZ, SLAB // NZ, BLK), bf16),
            pltpu.VMEM((SLAB // NZ, hid), f32),
            dma((6,)),
            dma((KINDS,)),
            dma((STEPS, NX)),
            dma((CHUNKS,)),
            dma,
            dma((CHUNKS,)),
            dma,
            dma,
            dma,
            dma,
            pltpu.SemaphoreType.REGULAR,
        ],
        compiler_params=pltpu.CompilerParams(
            collective_id=0, has_side_effects=True, vmem_limit_bytes=56 << 20
        ),
    )(
        features,
        order.reshape(1, SLAB),
        adj_values.reshape(RB * NZ * KB, BLK, BLK),
        adj_cols.transpose(2, 0, 1),
        adj_count,
        weight.reshape(CHUNKS, BLK, BLK),
    )


def solution(mesh):
    placed = (
        P("row", None),
        P("row"),
        P("row", "rep", None, None, None),
        P("row", "rep", None),
        P("row", "rep"),
        P(None, "rep"),
    )
    return jax.shard_map(
        shards, mesh=mesh, in_specs=placed, out_specs=P(("row", "rep"), None), check_vma=False
    )
```

time: 324 us -> 64.5 us (0.20); the launches traced: 320 us -> 64.1 us
  waiting for transfers between devices: 248 us -> 0 us
  Pallas kernels: 0 us -> 62.6 us
  local copies, waits for them, and re-layouts: 36.5 us -> 1.57 us
  between operations: 15.1 us -> 0.01 us
  matrix products: 12.5 us -> 0 us
  other arithmetic: 7.71 us -> 0 us
    psum x1 -> x0, waiting for transfers between devices: 207 us -> none  [broadcast(): return lax.psum(jnp.where(mine, x, jnp.zeros_like(x)), axis)]
    pallas_call x0 -> x1, Pallas kernels: none -> 62.6 us  [shards(): pl.pallas_call(kernel, out_shape=jax.ShapeDtypeStruct((SLAB // NZ, hid),...]
    reduce_scatter x1 -> x0, waiting for transfers between devices: 40.2 us -> none  [shards(): lax.psum_scatter(partial_orig, 'rep', scatter_dimension=0, tiled=True)]
    gather x10 -> x0, local copies, waits for them, and re-layouts: 28.3 us -> none  [the longest x8 23.6 us: shards(): chosen = pieces[adj_cols[:, section]]]
    dot_general x9 -> x0, matrix products: 12.5 us -> none  [the longest x8 9.97 us: shards(): jnp.einsum('rkij,rkjd->rid', masked[:, section], chosen, preferred_elemen...]
    mul x1 -> x0, other arithmetic: 3.83 us -> none  [shards(): masked = adj_values * live_slots[:, :, :, None, None]]
    select_n x7 -> x0, other arithmetic: 3.72 us -> none  [the longest x1 2.93 us: broadcast(): return lax.psum(jnp.where(mine, x, jnp.zeros_like(x)), axis)]
  transfers between devices with their start and end apart: 3 -> 0, of which waited for: 2 -> 0; matrix products, arithmetic and copies ran while one was open for 14% -> 0% of each run, Pallas kernels for 0% -> 0%
where the time goes in v2:
time: 64.5 us; the launch traced here: 64.1 us
  Pallas kernels  62.6 us (97%)
  local copies, waits for them, and re-layouts  1.57 us (2%)
    pallas_call x1, Pallas kernels, shards(): pl.pallas_call(kernel, out_shape=jax.ShapeDtypeStruct((SLAB // NZ, hid),...  62.6 us
    unnamed x1, local copies, waits for them, and re-layouts  1.57 us

profile of v2, /device:TPU:1, one launch (start us, length us, event | category | flops | bytes accessed | tf_op | source)
XLA Modules:
  0.0 64.1 jit_solution(674323225241833038)
XLA Ops:
  0.0 62.6 %shard_map.64 = bf16[64,1024]{1,0:T(8,128)(2,1)} custom-call(bf16[512,768]{1,0:T(8,128)(2,1)} %feat_hbm.1, s32[1,512]{1,0:T(1,128)} %bitcast.7, bf16[96,128,128]{2,1,0:T(8,128)(2,1)} %bitcast.4, s32[3,4,8]{2,1,0:T(4,128)} %bitcast.6, s32[4,8]{1,0:T(4,128)} %count_hbm.1, bf16[6,128,128]{2,1,0:T(8,128)(2,1)} %bitcast.5), custom_call_target="tpu_custom_call" | custom-call | tf_op jit(solution)/shard_map/pallas_call | solution.py:306
  62.6 1.6 %copy.8 = bf16[64,1024]{1,0:T(8,128)(2,1)} copy(bf16[64,1024]{1,0:T(8,128)(2,1)} %shard_map.64) | data formatting | bytes 262144

commit v3 on v2

--- a/solution.py
+++ b/solution.py
@@ -17,12 +17,12 @@
 SUB = 4
 ROWS = SLAB // SUB
 STEPS = CHUNKS * SUB
-PRE = 6
+PRE = 4
 LAG_X1 = 4
 LAG_X2 = 8
-LAG_COMPUTE = 12
+LAG_COMPUTE = 10
 ITERS = LAG_X2 + STEPS
-DIRECT = STEPS - SUB
+DIRECT = STEPS - 1
 READY_AT = 4
 WEIGHT_AT = 22
 YP1, YM1, YP2, YM2, XP, XM, XO, FR, FL, SIB = range(10)
@@ -80,21 +80,20 @@
     def unit(s, x0):
         return slabs.at[s // SUB, c * NX + x0, pl.ds((s % SUB) * ROWS, ROWS)]
 
+    def in_order(first, count):
+        ordered = lax.dot_general(
+            perm[...], feat[:, first * BLK:(first + count) * BLK], (((0,), (0,)), ((), ())),
+            preferred_element_type=jnp.float32,
+        ).astype(jnp.bfloat16)
+        for k in range(count):
+            slabs[first + k, c * NX + x] = ordered[:, k * BLK:(k + 1) * BLK]
+
     @pl.when(d == 0)
     def _():
         load_feat.wait()
-        ordered = lax.dot_general(
-            perm[...], feat[...], (((0,), (0,)), ((), ())), preferred_element_type=jnp.float32
-        ).astype(jnp.bfloat16)
-        for ch in range(CHUNKS):
-            slabs[ch, c * NX + x] = ordered[:, ch * BLK:(ch + 1) * BLK]
+        in_order(0, 1)
 
     pl.semaphore_wait(barrier, len(near) + rep)
-    for k in range(1, NZ):
-        @pl.when(rep >= k)
-        def _(k=k):
-            pl.semaphore_signal(ready, inc=1, device_id=(row, rep - k), device_id_type=MESH)
-
     def remote(src, dst, sent, landed, target):
         return pltpu.make_async_remote_copy(
             src_ref=src, dst_ref=dst, send_sem=sent, recv_sem=landed, device_id=target, device_id_type=MESH
@@ -103,8 +102,21 @@
     def copy_to(s, x0, kind, target):
         return remote(unit(s, x0), unit(s, x0), send_sem.at[kind], recv_sem.at[s, x0], target)
 
-    def copy_sib(s, x0):
-        return remote(unit(s, x0), unit(s, x0), send_sem.at[SIB], sib_sem.at[s // SUB], sibling)
+    def sib_sends(s, x0):
+        ch = s // SUB
+        whole = slabs.at[ch, c * NX + x0]
+
+        @pl.when((s % SUB == SUB - 1) & (ch < CHUNKS - 1))
+        def _():
+            remote(whole, whole, send_sem.at[SIB], sib_sem.at[ch, x0], sibling).start()
+
+        @pl.when(ch == CHUNKS - 1)
+        def _():
+            remote(unit(s, x0), unit(s, x0), send_sem.at[SIB], sib_sem.at[ch, x0], sibling).start()
+
+    def sib_arrive(ch, x0):
+        ref = slabs.at[ch, (1 - c) * NX + x0]
+        remote(ref, ref, send_sem.at[SIB], sib_sem.at[ch, x0], sibling).wait_recv()
 
     second = (d == 2) | (d == NY - 2)
 
@@ -119,12 +131,8 @@
         ref = w_all.at[:, mine]
         return remote(ref, ref, w_sib_send, w_sib_recv, sibling)
 
-    load_w.wait()
-    for k in (4, 3, 5, 2, 6, 1, 7):
-        pl.when(rep + k >= NZ)(w_copy(k).start)
-
     def own_step(s):
-        even = s % 2 == 0
+        even = (s + c) % 2 == 0
         for cond, kind, target in (
             ((d == 0) | ((d == 2) & even), YP2, up2),
             ((d == 0) | ((d == NY - 2) & jnp.logical_not(even)), YM2, down2),
@@ -135,13 +143,13 @@
         copy_to(s, x, XP, right).start()
         copy_to(s, x, XM, left).start()
         pl.when(s >= DIRECT)(copy_to(s, x, XO, opposite).start)
-        copy_sib(s, x).start()
+        sib_sends(s, x)
 
     def arrive(s, x0):
         copy_to(s, x0, XP, right).wait_recv()
 
-    def all_sent(kind, chunks):
-        ref = slabs.at[pl.ds(0, chunks), 0]
+    def all_sent(kind, units):
+        ref = slabs.at[0, :, pl.ds(0, units * (ROWS // (NC * NX)))]
         remote(ref, ref, send_sem.at[kind], w_recv, right).wait_send()
 
     def z_copy(ch, peer):
@@ -154,6 +162,16 @@
             return carry
 
         lax.fori_loop(0, PRE, first, 0)
+        in_order(1, CHUNKS - 1)
+
+    for k in range(1, NZ):
+        @pl.when(rep >= k)
+        def _(k=k):
+            pl.semaphore_signal(ready, inc=1, device_id=(row, rep - k), device_id_type=MESH)
+
+    load_w.wait()
+    for k in (4, 3, 5, 2, 6, 1, 7):
+        pl.when(rep + k >= NZ)(w_copy(k).start)
 
     adj[RB * NZ * KB] = jnp.zeros((BLK, BLK), jnp.bfloat16)
     load_cols.wait()
@@ -179,15 +197,22 @@
     def product(m, carry):
         ch, q = m // RB, m % RB
 
+        from_left, from_right, across = (x + NX - 1) % NX, (x + 1) % NX, (x + 2) % NX
+        x_a = jnp.where(q == 0, x, jnp.where(q == RB - 1, across, from_left))
+        x_b = jnp.where(q == 0, x, jnp.where(q == RB - 1, across, from_right))
+
         @pl.when(q == 2)
         def _():
-            ref = slabs.at[ch, pl.ds((1 - c) * NX, NX)]
-            remote(ref, ref, w_sib_send, sib_sem.at[ch], sibling).wait_recv()
-
-        layer = jnp.where(q < 2, c, 1 - c)
-        first = layer * NX + (q % 2) * 2
-        update = jnp.dot(dense[first], slabs[ch, first], preferred_element_type=jnp.float32) + jnp.dot(
-            dense[first + 1], slabs[ch, first + 1], preferred_element_type=jnp.float32
+            sib_arrive(ch, x_a)
+
+        @pl.when(q != 1)
+        def _():
+            sib_arrive(ch, x_b)
+
+        a = jnp.where(q == 2, 1 - c, c) * NX + x_a
+        b = jnp.where(q == 1, c, 1 - c) * NX + x_b
+        update = jnp.dot(dense[a], slabs[ch, a], preferred_element_type=jnp.float32) + jnp.dot(
+            dense[b], slabs[ch, b], preferred_element_type=jnp.float32
         )
 
         @pl.when(q == 0)
@@ -223,19 +248,19 @@
         def _():
             s = i - LAG_X1
             forward = s < DIRECT
-            to_right = s % 2 == 0
+            to_right = (s + c) % 2 == 0
             from_left, from_right = (x + NX - 1) % NX, (x + 1) % NX
             arrive(s, from_left)
             pl.when(forward & to_right)(copy_to(s, from_left, FR, right).start)
-            copy_sib(s, from_left).start()
+            sib_sends(s, from_left)
             arrive(s, from_right)
             pl.when(forward & jnp.logical_not(to_right))(copy_to(s, from_right, FL, left).start)
-            copy_sib(s, from_right).start()
+            sib_sends(s, from_right)
 
         @pl.when(i >= LAG_X2)
         def _():
             arrive(i - LAG_X2, (x + 2) % NX)
-            copy_sib(i - LAG_X2, (x + 2) % NX).start()
+            sib_sends(i - LAG_X2, (x + 2) % NX)
 
         @pl.when(i == READY_AT)
         def _():
@@ -252,37 +277,38 @@
             remote(ref, ref, w_send, w_recv, sibling).wait()
             w_sib().start()
 
-        @pl.when((i >= LAG_COMPUTE) & (i < LAG_COMPUTE + (CHUNKS - 1) * SUB))
-        def _():
-            at = (i - LAG_COMPUTE) * (RB // SUB)
-            lax.fori_loop(at, at + RB // SUB, product, 0)
+        @pl.when(i >= LAG_COMPUTE)
+        def _():
+            product(i - LAG_COMPUTE, 0)
 
         return carry
 
     lax.fori_loop(0, ITERS, iteration, 0)
-    lax.fori_loop((CHUNKS - 1) * RB, CHUNKS * RB, product, 0)
-
-    for kind in (XP, XM):
-        all_sent(kind, CHUNKS)
-    all_sent(XO, 1)
-    for kind in (FR, FL):
-        ref = slabs.at[0, pl.ds(0, CHUNKS - 1), pl.ds(0, SLAB // 2)]
-        remote(ref, ref, send_sem.at[kind], w_recv, right).wait_send()
+    lax.fori_loop(ITERS - LAG_COMPUTE, CHUNKS * RB, product, 0)
+
+    for kind, units in ((XP, STEPS), (XM, STEPS), (XO, STEPS - DIRECT)):
+        all_sent(kind, units)
+    for first, second_kind, core in ((FR, FL, 0), (FL, FR, 1)):
+        @pl.when(c == core)
+        def _(first=first, second_kind=second_kind):
+            all_sent(first, (DIRECT + 1) // 2)
+            all_sent(second_kind, DIRECT // 2)
+
     ref = slabs.at[:, pl.ds(0, NX)]
     remote(ref, ref, send_sem.at[SIB], w_recv, right).wait_send()
 
     @pl.when(d == 0)
     def _():
-        all_sent(YP2, CHUNKS)
-        all_sent(YM2, CHUNKS)
+        all_sent(YP2, STEPS)
+        all_sent(YM2, STEPS)
 
     @pl.when(second)
     def _():
-        all_sent(YP1, CHUNKS)
-        all_sent(YM1, CHUNKS)
-
-    pl.when(d == 2)(functools.partial(all_sent, YP2, CHUNKS // 2))
-    pl.when(d == NY - 2)(functools.partial(all_sent, YM2, CHUNKS // 2))
+        all_sent(YP1, STEPS)
+        all_sent(YM1, STEPS)
+
+    pl.when(d == 2)(functools.partial(all_sent, YP2, STEPS // 2))
+    pl.when(d == NY - 2)(functools.partial(all_sent, YM2, STEPS // 2))
     w_sib().wait()
 
     def finish(ch, carry):
@@ -325,7 +351,7 @@
             dma((6,)),
             dma((KINDS,)),
             dma((STEPS, NX)),
-            dma((CHUNKS,)),
+            dma((CHUNKS, NX)),
             dma,
             dma((CHUNKS,)),
             dma,

time: 64.5 us -> 62.2 us (0.964)
  Pallas kernels: 62.6 us -> 60.5 us
    pallas_call x1, Pallas kernels: 62.6 us -> 60.5 us  [shards(): pl.pallas_call(kernel, out_shape=jax.ShapeDtypeStruct((SLAB // NZ, hid),...]
where the time goes in v3:
time: 62.2 us; the launch traced here: 62 us
  Pallas kernels  60.5 us (97%)
  local copies, waits for them, and re-layouts  1.57 us (3%)
    pallas_call x1, Pallas kernels, shards(): pl.pallas_call(kernel, out_shape=jax.ShapeDtypeStruct((SLAB // NZ, hid),...  60.5 us
    unnamed x1, local copies, waits for them, and re-layouts  1.57 us

profile of v3, /device:TPU:1, one launch (start us, length us, event | category | flops | bytes accessed | tf_op | source)
XLA Modules:
  0.0 62.0 jit_solution(3208238288021230841)
XLA Ops:
  0.0 60.5 %shard_map.64 = bf16[64,1024]{1,0:T(8,128)(2,1)} custom-call(bf16[512,768]{1,0:T(8,128)(2,1)} %feat_hbm.1, s32[1,512]{1,0:T(1,128)} %bitcast.7, bf16[96,128,128]{2,1,0:T(8,128)(2,1)} %bitcast.4, s32[3,4,8]{2,1,0:T(4,128)} %bitcast.6, s32[4,8]{1,0:T(4,128)} %count_hbm.1, bf16[6,128,128]{2,1,0:T(8,128)(2,1)} %bitcast.5), custom_call_target="tpu_custom_call" | custom-call | tf_op jit(solution)/shard_map/pallas_call | solution.py:332
  60.5 1.6 %copy.8 = bf16[64,1024]{1,0:T(8,128)(2,1)} copy(bf16[64,1024]{1,0:T(8,128)(2,1)} %shard_map.64) | data formatting | bytes 262144

commit v4 on v3

--- a/solution.py
+++ b/solution.py
@@ -24,7 +24,7 @@
 ITERS = LAG_X2 + STEPS
 DIRECT = STEPS - 1
 READY_AT = 4
-WEIGHT_AT = 22
+WEIGHT_AT = 29
 YP1, YM1, YP2, YM2, XP, XM, XO, FR, FL, SIB = range(10)
 KINDS = SIB + 1
 

time: 62.2 us -> 62.2 us (level)
  no operation moved by 1% of the time
where the time goes in v4:
time: 62.2 us; the launch traced here: 62 us
  Pallas kernels  60.5 us (97%)
  local copies, waits for them, and re-layouts  1.57 us (3%)
    pallas_call x1, Pallas kernels, shards(): pl.pallas_call(kernel, out_shape=jax.ShapeDtypeStruct((SLAB // NZ, hid),...  60.5 us
    unnamed x1, local copies, waits for them, and re-layouts  1.57 us

profile of v4, /device:TPU:1, one launch (start us, length us, event | category | flops | bytes accessed | tf_op | source)
XLA Modules:
  0.0 62.0 jit_solution(8338493256350175670)
XLA Ops:
  0.0 60.5 %shard_map.64 = bf16[64,1024]{1,0:T(8,128)(2,1)} custom-call(bf16[512,768]{1,0:T(8,128)(2,1)} %feat_hbm.1, s32[1,512]{1,0:T(1,128)} %bitcast.7, bf16[96,128,128]{2,1,0:T(8,128)(2,1)} %bitcast.4, s32[3,4,8]{2,1,0:T(4,128)} %bitcast.6, s32[4,8]{1,0:T(4,128)} %count_hbm.1, bf16[6,128,128]{2,1,0:T(8,128)(2,1)} %bitcast.5), custom_call_target="tpu_custom_call" | custom-call | tf_op jit(solution)/shard_map/pallas_call | solution.py:332
  60.5 1.6 %copy.8 = bf16[64,1024]{1,0:T(8,128)(2,1)} copy(bf16[64,1024]{1,0:T(8,128)(2,1)} %shard_map.64) | data formatting | bytes 262144
